TPU v7x, 256 devices: a whole 4x4x8 slice. The times are simulated.
256 devices in a mesh: expert: 8 (over y, core), fsdp: 32 (over x, z).
Axes of the slice: x: 4, y: 4, z: 8, core: 2. Of those that a mesh axis runs over, the one named last changes fastest.
Arguments:
- tokens: bfloat16 [32768, 3072], P(('expert', 'fsdp')), may hold values from -6 to 6
- cotangent: bfloat16 [32768, 3072], P(('expert', 'fsdp')), may hold values from -6 to 6
- expert_ids: int32 [32768, 2], P(('expert', 'fsdp')), may hold values from 0 to 7, all different within a row; in each aligned block of 128 rows (0 to 127, 128 to 255, ...) at most 40 rows name the same one
- probs: bfloat16 [32768, 2], P(('expert', 'fsdp')), may hold values from 0.049804688 to 0.94921875
- gate_tiles: bfloat16 [8, 32, 128, 128], P('expert', 'fsdp'), may hold values from -0.5 to 0.5
- up_tiles: bfloat16 [8, 32, 128, 128], P('expert', 'fsdp'), may hold values from -0.5 to 0.5
- down_tiles: bfloat16 [8, 32, 128, 128], P('expert', 'fsdp'), may hold values from -0.5 to 0.5
- in_ids: int32 [8, 32], P('expert'), may hold values from 0 to 1535, as said below
- in_count: int32 [8, 32], P('expert'), may hold values from 0 to 1, as said below
- out_ids: int32 [8, 32], P('expert'), may hold values from 0 to 23
- out_count: int32 [8, 32], P('expert'), may hold values from 0 to 1, as said below
Outputs:
- token_grad: bfloat16 [32768, 3072], P(('expert', 'fsdp'))
- prob_grad: bfloat16 [32768, 2], P(('expert', 'fsdp'))
- gate_grad: float32 [8, 32, 128, 128], P('expert', 'fsdp')
- up_grad: float32 [8, 32, 128, 128], P('expert', 'fsdp')
- down_grad: float32 [8, 32, 128, 128], P('expert', 'fsdp')
Inputs may be any that keep to these rules, and one draw needn't show every extreme that they name: `expert_ids`: in each block of the rows of one device no expert is named more than 40 times. The column blocks in_ids % (64) of the 32 entries of one expert differ from one another. `in_count`: some device of each expert has all its slots live. `out_count`: some device of each expert has all its slots live.
All inputs are finite; a program needn't handle non-finite values.
Results may differ from a plain program's by a relative error of at most 0.0052.
Values may be sent and summed in bfloat16 or wider, within the bound.
No kernel may reach another device: no remote copies, remote signals or barrier semaphores. Data moves between devices by JAX's collectives and lax.ppermute only.
A program may use at most 128 MiB of HBM per device.

v0:
```python
import functools

import jax
import jax.numpy as jnp
from jax import lax
from jax.experimental import pallas as pl
from jax.experimental.pallas import tpu as pltpu
from jax.sharding import Mesh
from jax.sharding import PartitionSpec as P

FF = 8192
TILE = 128
COL_BLOCKS = FF // TILE
EXPERTS = 8
NX = 4
NZ = 8
SLOTS = NX * NZ
CAP = 40
ROWS = 128
WIDTH = 3072
TOTAL = EXPERTS * CAP
PEERS = EXPERTS * NX
AHEAD = 16
IN_AT, OUT_AT, Z_AT, COUNT_AT, RANK_AT, BRANCH_AT = range(6)
SIZES = (3, 4, 8)

BF = jnp.bfloat16
F32 = jnp.float32
SMEM = pl.BlockSpec(memory_space=pltpu.SMEM)
VMEM = pl.BlockSpec(memory_space=pltpu.VMEM)
HBM = pl.BlockSpec(memory_space=pltpu.HBM)
LIMIT = 40 * 1024 * 1024


def call(kernel, out, ins, outs, scratch=(), cost=None):
    return pl.pallas_call(
        kernel,
        out_shape=out,
        in_specs=ins,
        out_specs=outs,
        scratch_shapes=list(scratch),
        cost_estimate=cost,
        compiler_params=pltpu.CompilerParams(vmem_limit_bytes=LIMIT),
    )


def dot(a, b):
    return lax.dot_general(a, b, (((1,), (0,)), ((), ())), preferred_element_type=F32)


def dot_nt(a, b):
    return lax.dot_general(a, b, (((1,), (1,)), ((), ())), preferred_element_type=F32)


def dot_tn(a, b):
    return lax.dot_general(a, b, (((0,), (0,)), ((), ())), preferred_element_type=F32)


def lean(per):
    return per > 4


def block(j, size):
    if isinstance(j, int):
        return slice(j * size, (j + 1) * size)
    return pl.ds(pl.multiple_of(j * size, size), size)


def each(count, body, per):
    if lean(per):
        lax.fori_loop(0, count, lambda j, _: body(j) or 0, 0)
    else:
        for j in range(count):
            body(j)


def back_tail(per):
    return 16 if per % 2 == 0 else 8


def plan_kernel(counts, plan, copies):
    slot_i = lax.broadcasted_iota(jnp.int32, (SLOTS, SLOTS), 0)
    slot_j = lax.broadcasted_iota(jnp.int32, (SLOTS, SLOTS), 1)
    order_i = (slot_i & (NZ - 1)) * NX + (slot_i >> 3)
    order_j = (slot_j & (NZ - 1)) * NX + (slot_j >> 3)

    def column(line):
        return jnp.sum(jnp.where(slot_i == slot_j, line, 0.0), axis=1, keepdims=True)

    live = jnp.logical_and(counts[1:2, :] > 0, counts[3:4, :] > 0).astype(F32)
    rank = jnp.sum(jnp.where(order_j < order_i, live, 0.0), axis=1, keepdims=True)
    live_column = column(live)
    hot = jnp.logical_and(rank == slot_j.astype(F32), live_column > 0.0)

    def by_rank(values):
        return jnp.sum(jnp.where(hot, values, 0.0), axis=0, keepdims=True)

    rank_line = jnp.sum(jnp.where(order_i < order_j, live_column, 0.0), axis=0, keepdims=True)
    count = jnp.sum(live, axis=1, keepdims=True) + jnp.zeros_like(live)
    branch = jnp.zeros_like(live)
    for size in SIZES[:-1]:
        branch = branch + (count > NX * size).astype(F32)
    plan[...] = jnp.zeros_like(plan)
    for at, line in (
        (IN_AT, by_rank(column((counts[0:1, :] >> 6).astype(F32)))),
        (OUT_AT, by_rank(column(counts[2:3, :].astype(F32)))),
        (Z_AT, by_rank((slot_i & (NZ - 1)).astype(F32))),
        (COUNT_AT, count),
        (RANK_AT, jnp.where(live > 0.0, rank_line, -1.0)),
        (BRANCH_AT, branch),
    ):
        plan[at : at + 1, :SLOTS] = line.astype(jnp.int32)
    whole = plan[...]
    for e in range(EXPERTS):
        copies[e] = whole


def assignment(ids):
    experts = lax.broadcasted_iota(jnp.int32, (EXPERTS, ROWS), 0)
    first = ids[0:1, :] == experts
    second = ids[1:2, :] == experts
    named = jnp.logical_or(first, second)
    above = lax.broadcasted_iota(jnp.int32, (ROWS, ROWS), 0) < lax.broadcasted_iota(
        jnp.int32, (ROWS, ROWS), 1
    )
    place = dot(named.astype(F32).astype(BF), above.astype(F32).astype(BF))
    return first, second, jnp.where(named, place, -1.0)


def one_hot(place):
    at = lax.broadcasted_iota(jnp.int32, (CAP, ROWS), 0).astype(F32)
    rows = [(place[e : e + 1, :] == at).astype(F32) for e in range(EXPERTS)]
    return jnp.concatenate(rows, axis=0).astype(BF)


def dispatch_kernel(per, plans, ids, probs, tokens, cot, sent, xs, ys, prob_rows, places, out, sem):
    first, second, place = assignment(ids[...])
    p = probs[...].astype(F32)
    prob_rows[...] = jnp.where(first, p[0:1, :], 0.0) + jnp.where(second, p[1:2, :], 0.0)
    places[...] = place
    pick = one_hot(place)

    def gather(j):
        at = block(j, 256)
        xs[:, at] = dot(pick, tokens[:, at])
        ys[:, at] = dot(pick, cot[:, at])

    each(WIDTH // 256, gather, per)
    line = lax.broadcasted_iota(jnp.int32, (AHEAD, ROWS), 0)

    def per_expert(e, _):
        rows = pl.ds(pl.multiple_of(e * CAP, 8), CAP)
        extra = jnp.where(
            line == 0,
            prob_rows[pl.ds(e, 1), :],
            jnp.where(line == 1, places[pl.ds(e, 1), :], 0.0),
        ).astype(BF)
        for x in range(NX):
            for k in range(per):
                r = k * NX + x
                at_in = pl.multiple_of(plans[e, IN_AT, r] * TILE, TILE)
                at_out = pl.multiple_of(plans[e, OUT_AT, r] * TILE, TILE)
                both = jnp.concatenate(
                    [xs[rows, pl.ds(at_in, TILE)], ys[rows, pl.ds(at_out, TILE)]], axis=0
                )
                out[e * NX + x, 2 * CAP * k : 2 * CAP * (k + 1), :] = both.astype(BF)
            out[e * NX + x, 2 * CAP * per : 2 * CAP * per + AHEAD, :] = extra
        leave(e).start()
        return 0

    def leave(e):
        part = pl.ds(e * NX, NX)
        return pltpu.make_async_copy(out.at[part], sent.at[part], sem.at[e])

    def wait(e, _):
        leave(e).wait()
        return 0

    lax.fori_loop(0, EXPERTS, per_expert, 0)
    lax.fori_loop(0, EXPERTS, wait, 0)


def pick_weights_kernel(plan, place, own, one, two, three, out):
    x, z = place[0], place[1]
    out[...] = jnp.zeros_like(out)
    for shift, source in enumerate((own, one, two, three)):
        home = lax.rem(x + NX - shift, NX)
        rank = plan[RANK_AT, home * NZ + z]

        @pl.when(jnp.logical_and(rank >= 0, lax.rem(rank + NX, NX) == x))
        def _():
            out[...] = source[...]


def pick_grads_kernel(plan, place, own, one, two, three, gate, up, down):
    x, z = place[0], place[1]
    rank = plan[RANK_AT, x * NZ + z]
    outs = (gate, up, down)
    for ref in outs:
        ref[...] = jnp.zeros_like(ref)
    for shift, source in enumerate((own, one, two, three)):
        home = lax.rem(x + NX - shift, NX)

        @pl.when(jnp.logical_and(rank >= 0, lax.rem(rank + NX, NX) == home))
        def _():
            for i, ref in enumerate(outs):
                ref[0, 0] = source[i].astype(F32)


def expert_kernel(per, plan, place, got, weights, sent, *refs):
    outs, refs = refs[:NZ], refs[NZ:]
    pair, down, pair_sum, down_sum, back, kept, away, back_sem, grad_sem = refs
    x, own_z = place[0], place[1]
    count = plan[COUNT_AT, 0]
    for k in range(per):
        z = plan[Z_AT, k * NX + x]
        live = jnp.where(k * NX + x < count, 1.0, 0.0).astype(F32)
        for i in range(2):
            tile = weights[3 * z + i].astype(F32) * live
            pair[k, :, i * TILE : (i + 1) * TILE] = tile.astype(BF)
        down[k] = (weights[3 * z + 2].astype(F32) * live).astype(BF)
    pair_sum[...] = jnp.zeros_like(pair_sum)
    down_sum[...] = jnp.zeros_like(down_sum)
    group = 8
    rows = group * CAP
    tail = back_tail(per)
    ones = jnp.ones((ROWS, TILE), BF)

    def chunk(c, _):
        at = pl.ds(c * group, group)
        extra = got[at, 2 * CAP * per : 2 * CAP * per + AHEAD, :].astype(F32)
        slot = lax.broadcasted_iota(jnp.int32, (group, CAP, ROWS), 1).astype(F32)
        mine = extra[:, 1:2, :] == slot
        p = dot(jnp.where(mine, extra[:, 0:1, :], 0.0).reshape(rows, ROWS).astype(BF), ones)
        inner = jnp.zeros((rows, TILE), F32)
        pieces = []
        for k in range(per):
            both = got[at, 2 * CAP * k : 2 * CAP * (k + 1), :].astype(F32)
            rows_x = both[:, :CAP, :].reshape(rows, TILE).astype(BF)
            rows_dy = both[:, CAP:, :].reshape(rows, TILE)
            gu = dot(rows_x, pair[k])
            g, u = gu[:, :TILE], gu[:, TILE:]
            m = dot_nt(rows_dy.astype(BF), down[k])
            sig = jax.nn.sigmoid(g)
            act = g * sig
            h = (act * u).astype(BF)
            inner = inner + h.astype(F32) * m
            dh = p * m
            dg = (dh * u * sig * (1.0 + g * (1.0 - sig))).astype(BF)
            du = (dh * act).astype(BF)
            q = (p * rows_dy).astype(BF)
            dgu = jnp.concatenate([dg, du], axis=1)
            pieces.append(dot_nt(dgu, pair[k]).reshape(group, CAP, TILE))
            pair_sum[k] += dot_tn(rows_x, dgu)
            down_sum[k] += dot_tn(h, q)
        column = jnp.sum(inner, axis=1, keepdims=True).reshape(group, CAP, 1)
        row = jnp.sum(jnp.where(mine, column, 0.0), axis=1, keepdims=True)
        high = row.astype(BF).astype(F32)
        line = lax.broadcasted_iota(jnp.int32, (group, tail, ROWS), 1)
        pieces.append(jnp.where(line == 0, high, jnp.where(line == 1, row - high, 0.0)))
        back[at] = jnp.concatenate(pieces, axis=1).astype(BF)
        leave(c).start()
        return 0

    def leave(c):
        at = pl.ds(c * group, group)
        return pltpu.make_async_copy(back.at[at], sent.at[at], back_sem.at[c])

    def wait(c, _):
        leave(c).wait()
        return 0

    lax.fori_loop(0, PEERS // group, chunk, 0)
    kept[...] = jnp.zeros_like(kept)
    away[...] = jnp.zeros_like(away)
    for k in range(per):
        valid = k * NX + x < count
        shift = (plan[Z_AT, k * NX + x] - own_z) & (NZ - 1)

        @pl.when(jnp.logical_and(valid, shift == 0))
        def _():
            kept[0] = pair_sum[k, :, :TILE]
            kept[1] = pair_sum[k, :, TILE:]
            kept[2] = down_sum[k]

        @pl.when(jnp.logical_and(valid, shift > 0))
        def _():
            away[shift, 0] = pair_sum[k, :, :TILE].astype(BF)
            away[shift, 1] = pair_sum[k, :, TILE:].astype(BF)
            away[shift, 2] = down_sum[k].astype(BF)

    copies = [pltpu.make_async_copy(kept, outs[0], grad_sem.at[0])]
    for shift in range(1, NZ):
        copies.append(pltpu.make_async_copy(away.at[shift], outs[shift], grad_sem.at[shift]))
    for copy in copies:
        copy.start()
    for copy in copies:
        copy.wait()
    lax.fori_loop(0, PEERS // group, wait, 0)


def sum_kernel(own, *refs):
    total = own[...]
    for ref in refs[:-2]:
        total = total + ref[...].astype(F32)
    refs[-2][...] = total
    refs[-1][...] = total.astype(BF)


def combine_kernel(per, plans, ids, back, token_grad, prob_grad, parts, prob_rows):
    tail = back_tail(per)
    parts[...] = jnp.zeros_like(parts)

    def per_expert(e, _):
        rows = pl.ds(pl.multiple_of(e * CAP, 8), CAP)
        total = jnp.zeros((1, ROWS), F32)
        for x in range(NX):
            chunk = back[e * NX + x].astype(F32)
            for k in range(per):
                at = pl.multiple_of(plans[e, IN_AT, k * NX + x] * TILE, TILE)
                parts[rows, pl.ds(at, TILE)] += chunk[CAP * k : CAP * (k + 1), :]
            total = total + chunk[CAP * per : CAP * per + 1] + chunk[CAP * per + 1 : CAP * per + 2]
        prob_rows[pl.ds(e, 1), :] = total
        return 0

    lax.fori_loop(0, EXPERTS, per_expert, 0)
    first, second, place = assignment(ids[...])
    pick = one_hot(place)

    def gather(j):
        at = block(j, 256)
        token_grad[:, at] = dot_tn(pick, parts[:, at].astype(BF)).astype(BF)

    each(WIDTH // 256, gather, per)
    rows = prob_rows[...]
    prob_grad[...] = jnp.concatenate(
        [
            jnp.sum(jnp.where(first, rows, 0.0), axis=0, keepdims=True),
            jnp.sum(jnp.where(second, rows, 0.0), axis=0, keepdims=True),
        ],
        axis=0,
    ).astype(BF)


def exchange(values, axes):
    return lax.all_to_all(values, axes, split_axis=0, concat_axis=0, tiled=True)


def moved(values, axis, shift):
    size = lax.axis_size(axis)
    return lax.ppermute(values, axis, [(i, (i + shift) % size) for i in range(size)])


def rest(per, plan, plans, place, ids, probs, tokens, cotangent, *sources):
    shape = jax.ShapeDtypeStruct
    triple = (3, TILE, TILE)
    ahead = 2 * CAP * per + AHEAD
    behind = CAP * per + back_tail(per)
    sent = call(
        functools.partial(dispatch_kernel, per),
        pltpu.HBM((PEERS, ahead, TILE), BF),
        [SMEM, VMEM, VMEM, VMEM, VMEM],
        HBM,
        [
            pltpu.VMEM((TOTAL, WIDTH), F32),
            pltpu.VMEM((TOTAL, WIDTH), F32),
            pltpu.VMEM((EXPERTS, ROWS), F32),
            pltpu.VMEM((EXPERTS, ROWS), F32),
            pltpu.VMEM((PEERS, ahead, TILE), BF),
            pltpu.SemaphoreType.DMA((EXPERTS,)),
        ],
    )(plans, ids, probs, tokens, cotangent)
    got = exchange(sent, ("expert", "x"))
    weights = call(
        pick_weights_kernel,
        shape(triple, BF),
        [SMEM, SMEM, VMEM, VMEM, VMEM, VMEM],
        VMEM,
    )(plan, place, *sources)
    weights = lax.all_gather(weights, "z", axis=0, tiled=True)
    back, *grads = call(
        functools.partial(expert_kernel, per),
        (
            pltpu.HBM((PEERS, behind, TILE), BF),
            pltpu.HBM(triple, F32),
            *[pltpu.HBM(triple, BF)] * (NZ - 1),
        ),
        [SMEM, SMEM, VMEM, VMEM],
        [HBM] * (NZ + 1),
        [
            pltpu.VMEM((per, TILE, 2 * TILE), BF),
            pltpu.VMEM((per, TILE, TILE), BF),
            pltpu.VMEM((per, TILE, 2 * TILE), F32),
            pltpu.VMEM((per, TILE, TILE), F32),
            pltpu.VMEM((PEERS, behind, TILE), BF),
            pltpu.VMEM(triple, F32),
            pltpu.VMEM((NZ,) + triple, BF),
            pltpu.SemaphoreType.DMA((PEERS // 8,)),
            pltpu.SemaphoreType.DMA((NZ,)),
        ],
    )(plan, place, got, weights)
    returned = exchange(back, ("expert", "x"))
    if lean(per):
        ordered = jnp.roll(jnp.stack([term.astype(F32) for term in grads]), place[1], axis=0)
        own = jnp.sum(exchange(ordered, "z"), axis=0)
        whole = exchange(jnp.broadcast_to(own[None], (NX,) + triple), "x")
        nearby = [
            lax.dynamic_index_in_dim(whole, (place[0] + NX - shift) % NX, keepdims=False)
            for shift in range(1, NX)
        ]
    else:
        terms = [moved(grads[shift], "z", shift) for shift in (1, 7, 2, 6, 3, 5, 4)]
        own, sent = call(
            sum_kernel, (shape(triple, F32), shape(triple, BF)), [VMEM] * NZ, (VMEM, VMEM)
        )(grads[0], *terms)
        nearby = [moved(sent, "x", shift) for shift in range(1, NX)]
    token_grad, prob_grad = call(
        functools.partial(combine_kernel, per),
        (shape((ROWS, WIDTH), BF), shape((2, ROWS), BF)),
        [SMEM, VMEM, VMEM],
        (VMEM, VMEM),
        [pltpu.VMEM((TOTAL, WIDTH), F32), pltpu.VMEM((EXPERTS, ROWS), F32)],
        pl.CostEstimate(
            flops=2 * ROWS * TOTAL * WIDTH,
            bytes_accessed=3 * 4 * TOTAL * WIDTH + 2 * PEERS * behind * TILE,
            transcendentals=0,
        ),
    )(plans, ids, returned)
    token_grad, *nearby = lax.optimization_barrier((token_grad, *nearby))
    tile = shape((1, 1, TILE, TILE), F32)
    gate, up, down = call(
        pick_grads_kernel,
        (tile, tile, tile),
        [SMEM, SMEM, VMEM, VMEM, VMEM, VMEM],
        (VMEM, VMEM, VMEM),
    )(plan, place, own, *nearby)
    return token_grad, prob_grad, gate, up, down


def local(
    tokens,
    cotangent,
    expert_ids,
    probs,
    gate_tiles,
    up_tiles,
    down_tiles,
    in_ids,
    in_count,
    out_ids,
    out_count,
):
    shape = jax.ShapeDtypeStruct
    counts = jnp.concatenate([in_ids, in_count, out_ids, out_count], axis=0)
    plan, copies = call(
        plan_kernel,
        (shape((8, 128), jnp.int32), shape((EXPERTS, 8, 128), jnp.int32)),
        [VMEM],
        (VMEM, VMEM),
    )(counts)
    plans = exchange(copies, "expert")
    which = jnp.max(plans[:, BRANCH_AT, 0])
    place = jnp.stack([lax.axis_index("x"), lax.axis_index("z")]).astype(jnp.int32)
    ids = expert_ids.T
    rows = probs.T
    plan, *three = lax.optimization_barrier((plan, gate_tiles, up_tiles, down_tiles))
    own = jnp.concatenate([tile[0] for tile in three], axis=0)
    sources = [own] + [moved(own, "x", shift) for shift in range(1, NX)]
    token_grad, prob_grad, gate, up, down = lax.switch(
        which,
        [functools.partial(rest, size) for size in SIZES],
        plan,
        plans,
        place,
        ids,
        rows,
        tokens,
        cotangent,
        *sources,
    )
    return token_grad, prob_grad.T, gate, up, down


def solution(mesh):
    finer = Mesh(mesh.devices.reshape(EXPERTS, NX, NZ), ("expert", "x", "z"))
    rows = P(("expert", "x", "z"), None)
    tiles = P("expert", ("x", "z"), None, None)
    table = P("expert", None)
    return jax.shard_map(
        local,
        mesh=finer,
        in_specs=(rows, rows, rows, rows, tiles, tiles, tiles, table, table, table, table),
        out_specs=(rows, rows, tiles, tiles, tiles),
        check_vma=False,
    )
```

profile of v0, /device:TPU:32, one launch (start us, length us, event | category | flops | bytes accessed | tf_op | source)
XLA Modules:
  0.0 108.6 jit_solution(915883845381284104)
XLA Ops:
  2.9 1.6 %collective-permute-start.20 = (bf16[3,128,128]{2,1,0:T(8,128)(2,1)S(1)}, bf16[3,128,128]{2,1,0:T(8,128)(2,1)S(1)}, u32[]{:S(2)}, u32[]{:S(2)}) collective-permute-start(bf16[3,128,128]{2,1,0:T(8,128)(2,1)S(1)} %pad_maximum_fusion), channel_id=1, source_target_pairs={{0,8},{8,16},{16,24},{24,0},{1,9},{9,17},{17,25},{25,1},{2,10},{10... | collective-permute-start | bytes 294920 | tf_op jit(solution)/shard_map/ppermute | solution.py:351
  4.5 2.7 %collective-permute-start.21 = (bf16[3,128,128]{2,1,0:T(8,128)(2,1)S(1)}, bf16[3,128,128]{2,1,0:T(8,128)(2,1)S(1)}, u32[]{:S(2)}, u32[]{:S(2)}) collective-permute-start(bf16[3,128,128]{2,1,0:T(8,128)(2,1)S(1)} %pad_maximum_fusion), channel_id=1, source_target_pairs={{0,16},{8,24},{16,0},{24,8},{1,17},{9,25},{17,1},{25,9},{2,18},{10... | collective-permute-start | bytes 294920 | tf_op jit(solution)/shard_map/ppermute | solution.py:351
  7.2 1.4 %collective-permute-start.22 = (bf16[3,128,128]{2,1,0:T(8,128)(2,1)S(1)}, bf16[3,128,128]{2,1,0:T(8,128)(2,1)S(1)}, u32[]{:S(2)}, u32[]{:S(2)}) collective-permute-start(bf16[3,128,128]{2,1,0:T(8,128)(2,1)S(1)} %pad_maximum_fusion), channel_id=1, source_target_pairs={{0,24},{8,0},{16,8},{24,16},{1,25},{9,1},{17,9},{25,17},{2,26},{10... | collective-permute-start | bytes 294920 | tf_op jit(solution)/shard_map/ppermute | solution.py:351
  8.6 4.5 %all-to-all-start.8 = ((s32[8,8,128]{2,1,0:T(8,128)}), s32[8,8,128]{2,1,0:T(8,128)S(1)}, u32[]{:S(2)}, u32[]{:S(2)}) async-start(s32[8,8,128]{2,1,0:T(8,128)} %get-tuple-element.179), calls=%async_computation.8 | async-start | bytes 65536 | tf_op jit(solution)/shard_map/all_to_all | solution.py:346
  13.2 5.4 %all-to-all-done.8 = s32[8,8,128]{2,1,0:T(8,128)S(1)} async-done(((s32[8,8,128]{2,1,0:T(8,128)}), s32[8,8,128]{2,1,0:T(8,128)S(1)}, u32[]{:S(2)}, u32[]{:S(2)}) %all-to-all-start.8) | async-done | bytes 32800 | tf_op jit(solution)/shard_map/all_to_all | solution.py:346
  19.9 88.2 %conditional.1 = (bf16[128,3072]{1,0:T(8,128)(2,1)}, bf16[2,128]{1,0:T(2,128)(2,1)S(1)}, f32[1,1,128,128]{3,2,1,0:T(8,128)}, f32[1,1,128,128]{3,2,1,0:T(8,128)}, f32[1,1,128,128]{3,2,1,0:T(8,128)}) conditional(s32[]{:T(128)} %clamp.3, (s32[8,8,128]{2,1,0:T(8,128)S(1)}, s32[2,128]{1,0:T(2,128)}, bf16[2,128]{1,0:T(2,128)(2,1)}, ...), branch_computations={%region_1.0_spmd, %region_2.0_spmd, %region_3.5_spmd} | conditional | flops 252690432 | bytes 59937768 | solution.py:469
  19.9 4.2 %branch_0_fun.6 = bf16[32,256,128]{2,1,0:T(8,128)(2,1)} custom-call(s32[8,8,128]{2,1,0:T(8,128)S(1)} %get-tuple-element.70.plans, s32[2,128]{1,0:T(2,128)} %get-tuple-element.71.ids, bf16[2,128]{1,0:T(2,128)(2,1)} %get-tuple-element.74.probs, bf16[128,3072]{1,0:T(8,128)(2,1)} %get-tuple-element.75.tokens, bf16[128,3072]{1,0:T(8,128)(2,1)} %get-tuple-element.76.cot), custom_call_target="tpu_custom_call" | custom-call | tf_op jit(solution)/shard_map/cond/branch_0_fun/pallas_call | solution.py:359
  24.1 4.0 %all-to-all-start = ((bf16[32,256,128]{2,1,0:T(8,128)(2,1)}), bf16[32,256,128]{2,1,0:T(8,128)(2,1)S(1)}, u32[]{:S(2)}, u32[]{:S(2)}) async-start(bf16[32,256,128]{2,1,0:T(8,128)(2,1)} %branch_0_fun.6), calls=%async_computation | async-start | bytes 4194304 | tf_op jit(solution)/shard_map/cond/branch_0_fun/all_to_all | solution.py:346
  28.8 28.8 %all_gather.6.weights = bf16[24,128,128]{2,1,0:T(8,128)(2,1)S(1)} all-gather(bf16[3,128,128]{2,1,0:T(8,128)(2,1)S(1)} %branch_0_fun.7), channel_id=1, replica_groups=mesh['expert'=8,'x'=4,'z'=8] {'z'}, dimensions={0}, use_global_device_ids=true | all-gather | bytes 884736 | tf_op jit(solution)/shard_map/cond/branch_0_fun/all_gather | solution.py:380
  57.6 6.2 %branch_0_fun.8 = (bf16[32,128,128]{2,1,0:T(8,128)(2,1)}, f32[3,128,128]{2,1,0:T(8,128)}, bf16[3,128,128]{2,1,0:T(8,128)(2,1)}, bf16[3,128,128]{2,1,0:T(8,128)(2...) custom-call(s32[8,128]{1,0:T(8,128)S(1)} %get-tuple-element.72.plan,, ...), custom_call_target="tpu_custom_call" | custom-call | tf_op jit(solution)/shard_map/cond/branch_0_fun/pallas_call | solution.py:381
  63.8 7.4 %all-to-all-start.1 = ((bf16[32,128,128]{2,1,0:T(8,128)(2,1)}), bf16[32,128,128]{2,1,0:T(8,128)(2,1)S(1)}, u32[]{:S(2)}, u32[]{:S(2)}) async-start(bf16[32,128,128]{2,1,0:T(8,128)(2,1)} %get-tuple-element.81), calls=%async_computation.1 | async-start | bytes 2097152 | tf_op jit(solution)/shard_map/cond/branch_0_fun/all_to_all | solution.py:346
  71.1 1.2 %collective-permute-start = (bf16[3,128,128]{2,1,0:T(8,128)(2,1)}, bf16[3,128,128]{2,1,0:T(8,128)(2,1)S(1)}, u32[]{:S(2)}, u32[]{:S(2)}) collective-permute-start(bf16[3,128,128]{2,1,0:T(8,128)(2,1)} %get-tuple-element.84), channel_id=1, source_target_pairs={{0,1},{1,2},{2,3},{3,4},{4,5},{5,6},{6,7},{7,0},{8,9},{9,10},{10,1... | collective-permute-start | bytes 294920 | tf_op jit(solution)/shard_map/cond/branch_0_fun/ppermute | solution.py:351
  73.2 1.8 %collective-permute-start.2 = (bf16[3,128,128]{2,1,0:T(8,128)(2,1)}, bf16[3,128,128]{2,1,0:T(8,128)(2,1)S(1)}, u32[]{:S(2)}, u32[]{:S(2)}) collective-permute-start(bf16[3,128,128]{2,1,0:T(8,128)(2,1)} %get-tuple-element.86), channel_id=1, source_target_pairs={{0,2},{1,3},{2,4},{3,5},{4,6},{5,7},{6,0},{7,1},{8,10},{9,11},{10,... | collective-permute-start | bytes 294920 | tf_op jit(solution)/shard_map/cond/branch_0_fun/ppermute | solution.py:351
  75.1 2.3 %collective-permute-start.3 = (bf16[3,128,128]{2,1,0:T(8,128)(2,1)}, bf16[3,128,128]{2,1,0:T(8,128)(2,1)S(1)}, u32[]{:S(2)}, u32[]{:S(2)}) collective-permute-start(bf16[3,128,128]{2,1,0:T(8,128)(2,1)} %get-tuple-element.87), channel_id=1, source_target_pairs={{0,6},{1,7},{2,0},{3,1},{4,2},{5,3},{6,4},{7,5},{8,14},{9,15},{10,... | collective-permute-start | bytes 294920 | tf_op jit(solution)/shard_map/cond/branch_0_fun/ppermute | solution.py:351
  77.4 4.5 %collective-permute-start.4 = (bf16[3,128,128]{2,1,0:T(8,128)(2,1)}, bf16[3,128,128]{2,1,0:T(8,128)(2,1)S(1)}, u32[]{:S(2)}, u32[]{:S(2)}) collective-permute-start(bf16[3,128,128]{2,1,0:T(8,128)(2,1)} %get-tuple-element.88), channel_id=1, source_target_pairs={{0,3},{1,4},{2,5},{3,6},{4,7},{5,0},{6,1},{7,2},{8,11},{9,12},{10,... | collective-permute-start | bytes 294920 | tf_op jit(solution)/shard_map/cond/branch_0_fun/ppermute | solution.py:351
  82.4 2.8 %collective-permute-start.6 = (bf16[3,128,128]{2,1,0:T(8,128)(2,1)}, bf16[3,128,128]{2,1,0:T(8,128)(2,1)S(1)}, u32[]{:S(2)}, u32[]{:S(2)}) collective-permute-start(bf16[3,128,128]{2,1,0:T(8,128)(2,1)} %get-tuple-element.90), channel_id=1, source_target_pairs={{0,4},{1,5},{2,6},{3,7},{4,0},{5,1},{6,2},{7,3},{8,12},{9,13},{10,... | collective-permute-start | bytes 294920 | tf_op jit(solution)/shard_map/cond/branch_0_fun/ppermute | solution.py:351
  85.2 0.9 collective-permute-done.4.refs_4_
  86.1 10.1 %collective-permute-done.5.refs_5_ = bf16[3,128,128]{2,1,0:T(8,128)(2,1)S(1)} collective-permute-done((bf16[3,128,128]{2,1,0:T(8,128)(2,1)}, bf16[3,128,128]{2,1,0:T(8,128)(2,1)S(1)}, u32[]{:S(2)}, u32[]{:S(2)}) %collective-permute-start.5) | collective-permute-done | bytes 98336 | tf_op jit(solution)/shard_map/cond/branch_0_fun/ppermute | solution.py:351
  96.2 0.9 copy-done
  97.3 1.9 %collective-permute-start.7 = (bf16[3,128,128]{2,1,0:T(8,128)(2,1)S(1)}, bf16[3,128,128]{2,1,0:T(8,128)(2,1)S(1)}, u32[]{:S(2)}, u32[]{:S(2)}) collective-permute-start(bf16[3,128,128]{2,1,0:T(8,128)(2,1)S(1)} %get-tuple-element.91), channel_id=1, source_target_pairs={{0,8},{8,16},{16,24},{24,0},{1,9},{9,17},{17,25},{25,1},{2,10},{10... | collective-permute-start | bytes 294920 | tf_op jit(solution)/shard_map/cond/branch_0_fun/ppermute | solution.py:351
  99.1 2.7 %collective-permute-start.8 = (bf16[3,128,128]{2,1,0:T(8,128)(2,1)S(1)}, bf16[3,128,128]{2,1,0:T(8,128)(2,1)S(1)}, u32[]{:S(2)}, u32[]{:S(2)}) collective-permute-start(bf16[3,128,128]{2,1,0:T(8,128)(2,1)S(1)} %get-tuple-element.91), channel_id=1, source_target_pairs={{0,16},{8,24},{16,0},{24,8},{1,17},{9,25},{17,1},{25,9},{2,18},{10... | collective-permute-start | bytes 294920 | tf_op jit(solution)/shard_map/cond/branch_0_fun/ppermute | solution.py:351
  101.8 1.5 %collective-permute-start.9 = (bf16[3,128,128]{2,1,0:T(8,128)(2,1)S(1)}, bf16[3,128,128]{2,1,0:T(8,128)(2,1)S(1)}, u32[]{:S(2)}, u32[]{:S(2)}) collective-permute-start(bf16[3,128,128]{2,1,0:T(8,128)(2,1)S(1)} %get-tuple-element.91), channel_id=1, source_target_pairs={{0,24},{8,0},{16,8},{24,16},{1,25},{9,1},{17,9},{25,17},{2,26},{10... | collective-permute-start | bytes 294920 | tf_op jit(solution)/shard_map/cond/branch_0_fun/ppermute | solution.py:351
  103.3 3.5 %branch_0_fun.9 = (bf16[128,3072]{1,0:T(8,128)(2,1)}, bf16[2,128]{1,0:T(2,128)(2,1)S(1)}) custom-call(s32[8,8,128]{2,1,0:T(8,128)S(1)} %get-tuple-element.70.plans, s32[2,128]{1,0:T(2,128)S(1)} %copy-done.12, bf16[32,128,128]{2,1,0:T(8,128)(2,1)S(1)} %all-to-all-done.1.back), custom_call_target="tpu_custom_call" | custom-call | flops 251658240 | bytes 12845056 | tf_op jit(solution)/shard_map/cond/branch_0_fun/pallas_call | solution.py:417
  106.8 1.3 %branch_0_fun.11 = (f32[1,1,128,128]{3,2,1,0:T(8,128)}, f32[1,1,128,128]{3,2,1,0:T(8,128)}, f32[1,1,128,128]{3,2,1,0:T(8,128)}) custom-call(s32[8,128]{1,0:T(8,128)S(1)} %get-tuple-element.72.plan, s32[2]{0:T(128)S(1)} %get-tuple-element.73.place, f32[3,128,128]{2,1,0:T(8,128)S(1)} %get-tuple-element.94.own, ...), custom_call_target="tpu_custom_call" | custom-call | tf_op jit(solution)/shard_map/cond/branch_0_fun/pallas_call | solution.py:431
  (27 shorter events, 5.7 us)
Async XLA Ops:
  2.9 16.9 %collective-permute-start.20 = (bf16[3,128,128]{2,1,0:T(8,128)(2,1)S(1)}, bf16[3,128,128]{2,1,0:T(8,128)(2,1)S(1)}, u32[]{:S(2)}, u32[]{:S(2)}) collective-permute-start(bf16[3,128,128]{2,1,0:T(8,128)(2,1)S(1)} %pad_maximum_fusion), channel_id=1, source_target_pairs={{0,8},{8,16},{16,24},{24,0},{1,9},{9,17},{17,25},{25,1},{2,10},{10... | collective-permute-start | bytes 294920 | tf_op jit(solution)/shard_map/ppermute | solution.py:351
  4.5 15.4 %collective-permute-start.21 = (bf16[3,128,128]{2,1,0:T(8,128)(2,1)S(1)}, bf16[3,128,128]{2,1,0:T(8,128)(2,1)S(1)}, u32[]{:S(2)}, u32[]{:S(2)}) collective-permute-start(bf16[3,128,128]{2,1,0:T(8,128)(2,1)S(1)} %pad_maximum_fusion), channel_id=1, source_target_pairs={{0,16},{8,24},{16,0},{24,8},{1,17},{9,25},{17,1},{25,9},{2,18},{10... | collective-permute-start | bytes 294920 | tf_op jit(solution)/shard_map/ppermute | solution.py:351
  7.2 12.7 %collective-permute-start.22 = (bf16[3,128,128]{2,1,0:T(8,128)(2,1)S(1)}, bf16[3,128,128]{2,1,0:T(8,128)(2,1)S(1)}, u32[]{:S(2)}, u32[]{:S(2)}) collective-permute-start(bf16[3,128,128]{2,1,0:T(8,128)(2,1)S(1)} %pad_maximum_fusion), channel_id=1, source_target_pairs={{0,24},{8,0},{16,8},{24,16},{1,25},{9,1},{17,9},{25,17},{2,26},{10... | collective-permute-start | bytes 294920 | tf_op jit(solution)/shard_map/ppermute | solution.py:351
  8.6 9.9 %all-to-all-start.8 = ((s32[8,8,128]{2,1,0:T(8,128)}), s32[8,8,128]{2,1,0:T(8,128)S(1)}, u32[]{:S(2)}, u32[]{:S(2)}) async-start(s32[8,8,128]{2,1,0:T(8,128)} %get-tuple-element.179), calls=%async_computation.8 | async-start | bytes 65536 | tf_op jit(solution)/shard_map/all_to_all | solution.py:346
  24.1 33.5 %all-to-all-start = ((bf16[32,256,128]{2,1,0:T(8,128)(2,1)}), bf16[32,256,128]{2,1,0:T(8,128)(2,1)S(1)}, u32[]{:S(2)}, u32[]{:S(2)}) async-start(bf16[32,256,128]{2,1,0:T(8,128)(2,1)} %branch_0_fun.6), calls=%async_computation | async-start | bytes 4194304 | tf_op jit(solution)/shard_map/cond/branch_0_fun/all_to_all | solution.py:346
  57.6 45.7 %copy-start.12 = (s32[2,128]{1,0:T(2,128)S(1)}, s32[2,128]{1,0:T(2,128)}, u32[]{:S(2)}) copy-start(s32[2,128]{1,0:T(2,128)} %get-tuple-element.71.ids) | copy-start | bytes 3076 | tf_op jit(solution)/shard_map/cond
  63.8 39.5 %all-to-all-start.1 = ((bf16[32,128,128]{2,1,0:T(8,128)(2,1)}), bf16[32,128,128]{2,1,0:T(8,128)(2,1)S(1)}, u32[]{:S(2)}, u32[]{:S(2)}) async-start(bf16[32,128,128]{2,1,0:T(8,128)(2,1)} %get-tuple-element.81), calls=%async_computation.1 | async-start | bytes 2097152 | tf_op jit(solution)/shard_map/cond/branch_0_fun/all_to_all | solution.py:346
  71.1 10.7 %collective-permute-start = (bf16[3,128,128]{2,1,0:T(8,128)(2,1)}, bf16[3,128,128]{2,1,0:T(8,128)(2,1)S(1)}, u32[]{:S(2)}, u32[]{:S(2)}) collective-permute-start(bf16[3,128,128]{2,1,0:T(8,128)(2,1)} %get-tuple-element.84), channel_id=1, source_target_pairs={{0,1},{1,2},{2,3},{3,4},{4,5},{5,6},{6,7},{7,0},{8,9},{9,10},{10,1... | collective-permute-start | bytes 294920 | tf_op jit(solution)/shard_map/cond/branch_0_fun/ppermute | solution.py:351
  72.4 10.0 %collective-permute-start.1 = (bf16[3,128,128]{2,1,0:T(8,128)(2,1)}, bf16[3,128,128]{2,1,0:T(8,128)(2,1)S(1)}, u32[]{:S(2)}, u32[]{:S(2)}) collective-permute-start(bf16[3,128,128]{2,1,0:T(8,128)(2,1)} %get-tuple-element.85), channel_id=1, source_target_pairs={{0,7},{1,0},{2,1},{3,2},{4,3},{5,4},{6,5},{7,6},{8,15},{9,8},{10,9... | collective-permute-start | bytes 294920 | tf_op jit(solution)/shard_map/cond/branch_0_fun/ppermute | solution.py:351
  73.2 12.0 %collective-permute-start.2 = (bf16[3,128,128]{2,1,0:T(8,128)(2,1)}, bf16[3,128,128]{2,1,0:T(8,128)(2,1)S(1)}, u32[]{:S(2)}, u32[]{:S(2)}) collective-permute-start(bf16[3,128,128]{2,1,0:T(8,128)(2,1)} %get-tuple-element.86), channel_id=1, source_target_pairs={{0,2},{1,3},{2,4},{3,5},{4,6},{5,7},{6,0},{7,1},{8,10},{9,11},{10,... | collective-permute-start | bytes 294920 | tf_op jit(solution)/shard_map/cond/branch_0_fun/ppermute | solution.py:351
  75.1 10.2 %collective-permute-start.3 = (bf16[3,128,128]{2,1,0:T(8,128)(2,1)}, bf16[3,128,128]{2,1,0:T(8,128)(2,1)S(1)}, u32[]{:S(2)}, u32[]{:S(2)}) collective-permute-start(bf16[3,128,128]{2,1,0:T(8,128)(2,1)} %get-tuple-element.87), channel_id=1, source_target_pairs={{0,6},{1,7},{2,0},{3,1},{4,2},{5,3},{6,4},{7,5},{8,14},{9,15},{10,... | collective-permute-start | bytes 294920 | tf_op jit(solution)/shard_map/cond/branch_0_fun/ppermute | solution.py:351
  77.4 8.7 %collective-permute-start.4 = (bf16[3,128,128]{2,1,0:T(8,128)(2,1)}, bf16[3,128,128]{2,1,0:T(8,128)(2,1)S(1)}, u32[]{:S(2)}, u32[]{:S(2)}) collective-permute-start(bf16[3,128,128]{2,1,0:T(8,128)(2,1)} %get-tuple-element.88), channel_id=1, source_target_pairs={{0,3},{1,4},{2,5},{3,6},{4,7},{5,0},{6,1},{7,2},{8,11},{9,12},{10,... | collective-permute-start | bytes 294920 | tf_op jit(solution)/shard_map/cond/branch_0_fun/ppermute | solution.py:351
  81.9 14.4 %collective-permute-start.5 = (bf16[3,128,128]{2,1,0:T(8,128)(2,1)}, bf16[3,128,128]{2,1,0:T(8,128)(2,1)S(1)}, u32[]{:S(2)}, u32[]{:S(2)}) collective-permute-start(bf16[3,128,128]{2,1,0:T(8,128)(2,1)} %get-tuple-element.89), channel_id=1, source_target_pairs={{0,5},{1,6},{2,7},{3,0},{4,1},{5,2},{6,3},{7,4},{8,13},{9,14},{10,... | collective-permute-start | bytes 294920 | tf_op jit(solution)/shard_map/cond/branch_0_fun/ppermute | solution.py:351
  82.4 13.8 %collective-permute-start.6 = (bf16[3,128,128]{2,1,0:T(8,128)(2,1)}, bf16[3,128,128]{2,1,0:T(8,128)(2,1)S(1)}, u32[]{:S(2)}, u32[]{:S(2)}) collective-permute-start(bf16[3,128,128]{2,1,0:T(8,128)(2,1)} %get-tuple-element.90), channel_id=1, source_target_pairs={{0,4},{1,5},{2,6},{3,7},{4,0},{5,1},{6,2},{7,3},{8,12},{9,13},{10,... | collective-permute-start | bytes 294920 | tf_op jit(solution)/shard_map/cond/branch_0_fun/ppermute | solution.py:351
  96.2 0.9 copy-start
  97.3 9.5 %collective-permute-start.7 = (bf16[3,128,128]{2,1,0:T(8,128)(2,1)S(1)}, bf16[3,128,128]{2,1,0:T(8,128)(2,1)S(1)}, u32[]{:S(2)}, u32[]{:S(2)}) collective-permute-start(bf16[3,128,128]{2,1,0:T(8,128)(2,1)S(1)} %get-tuple-element.91), channel_id=1, source_target_pairs={{0,8},{8,16},{16,24},{24,0},{1,9},{9,17},{17,25},{25,1},{2,10},{10... | collective-permute-start | bytes 294920 | tf_op jit(solution)/shard_map/cond/branch_0_fun/ppermute | solution.py:351
  99.1 7.7 %collective-permute-start.8 = (bf16[3,128,128]{2,1,0:T(8,128)(2,1)S(1)}, bf16[3,128,128]{2,1,0:T(8,128)(2,1)S(1)}, u32[]{:S(2)}, u32[]{:S(2)}) collective-permute-start(bf16[3,128,128]{2,1,0:T(8,128)(2,1)S(1)} %get-tuple-element.91), channel_id=1, source_target_pairs={{0,16},{8,24},{16,0},{24,8},{1,17},{9,25},{17,1},{25,9},{2,18},{10... | collective-permute-start | bytes 294920 | tf_op jit(solution)/shard_map/cond/branch_0_fun/ppermute | solution.py:351
  101.8 5.0 %collective-permute-start.9 = (bf16[3,128,128]{2,1,0:T(8,128)(2,1)S(1)}, bf16[3,128,128]{2,1,0:T(8,128)(2,1)S(1)}, u32[]{:S(2)}, u32[]{:S(2)}) collective-permute-start(bf16[3,128,128]{2,1,0:T(8,128)(2,1)S(1)} %get-tuple-element.91), channel_id=1, source_target_pairs={{0,24},{8,0},{16,8},{24,16},{1,25},{9,1},{17,9},{25,17},{2,26},{10... | collective-permute-start | bytes 294920 | tf_op jit(solution)/shard_map/cond/branch_0_fun/ppermute | solution.py:351
  108.1 0.5 copy-start.15
where the time goes:
time: 109 us
  starting transfers between devices  41.7 us (38%)
  blocking collectives  28.8 us (26%)
  Pallas kernels  16.7 us (15%)
  waiting for transfers between devices  16.4 us (15%)
  other arithmetic  2.23 us (2%)
  local copies, waits for them, and re-layouts  1.44 us (1%)
  between operations  1.32 us (1%)
    all_gather x1, blocking collectives, rest(): weights = lax.all_gather(weights, 'z', axis=0, tiled=True)  28.8 us
    ppermute x13, starting transfers between devices, moved(): lax.ppermute(values, axis, [(i, (i + shift) % size) for i in range(size)])  25.8 us
    all_to_all x3, starting transfers between devices, exchange(): return lax.all_to_all(values, axes, split_axis=0, concat_axis=0, tiled=True)  15.9 us
    ppermute x13, waiting for transfers between devices, moved(): lax.ppermute(values, axis, [(i, (i + shift) % size) for i in range(size)])  11 us
    pallas_call x1, Pallas kernels, rest(): call(functools.partial(expert_kernel, per), (pltpu.HBM((PEERS, behind, TI...  6.18 us
    all_to_all x3, waiting for transfers between devices, exchange(): return lax.all_to_all(values, axes, split_axis=0, concat_axis=0, tiled=True)  5.38 us
    pallas_call x1, Pallas kernels, rest(): call(functools.partial(dispatch_kernel, per), pltpu.HBM((PEERS, ahead, TI...  4.18 us
    pallas_call x1, Pallas kernels, rest(): call(functools.partial(combine_kernel, per), (shape((ROWS, WIDTH), BF), s...  3.5 us
  transfers between devices with their start and end apart: 16, of which 3 were waited for; matrix products, arithmetic and copies ran while one was open for 1% of the time, Pallas kernels for 4%

commit v1 on v0

--- a/solution.py
+++ b/solution.py
@@ -23,6 +23,8 @@
 AHEAD = 16
 IN_AT, OUT_AT, Z_AT, COUNT_AT, RANK_AT, BRANCH_AT = range(6)
 SIZES = (3, 4, 8)
+CHUNKS = (1, 4, 7, 5, 2, 3, 6)
+WAVES = ((0, 2), (2, 2), (4, 1), (5, 2))
 
 BF = jnp.bfloat16
 F32 = jnp.float32
@@ -208,7 +210,7 @@
 
 
 def expert_kernel(per, plan, place, got, weights, sent, *refs):
-    outs, refs = refs[:NZ], refs[NZ:]
+    outs, refs = refs[: len(WAVES) + 1], refs[len(WAVES) + 1 :]
     pair, down, pair_sum, down_sum, back, kept, away, back_sem, grad_sem = refs
     x, own_z = place[0], place[1]
     count = plan[COUNT_AT, 0]
@@ -277,21 +279,26 @@
         valid = k * NX + x < count
         shift = (plan[Z_AT, k * NX + x] - own_z) & (NZ - 1)
 
+        away_from_here = shift > 0
+
         @pl.when(jnp.logical_and(valid, shift == 0))
         def _():
             kept[0] = pair_sum[k, :, :TILE]
             kept[1] = pair_sum[k, :, TILE:]
             kept[2] = down_sum[k]
 
-        @pl.when(jnp.logical_and(valid, shift > 0))
+        shift = sum(jnp.where(shift == s, i, 0) for i, s in enumerate(CHUNKS))
+
+        @pl.when(jnp.logical_and(valid, away_from_here))
         def _():
             away[shift, 0] = pair_sum[k, :, :TILE].astype(BF)
             away[shift, 1] = pair_sum[k, :, TILE:].astype(BF)
             away[shift, 2] = down_sum[k].astype(BF)
 
     copies = [pltpu.make_async_copy(kept, outs[0], grad_sem.at[0])]
-    for shift in range(1, NZ):
-        copies.append(pltpu.make_async_copy(away.at[shift], outs[shift], grad_sem.at[shift]))
+    for i, (start, size) in enumerate(WAVES):
+        part = away.at[start : start + size]
+        copies.append(pltpu.make_async_copy(part, outs[i + 1], grad_sem.at[i + 1]))
     for copy in copies:
         copy.start()
     for copy in copies:
@@ -299,10 +306,15 @@
     lax.fori_loop(0, PEERS // group, wait, 0)
 
 
-def sum_kernel(own, *refs):
-    total = own[...]
+def relay_kernel(stay, below, above, up, down):
+    up[...] = (stay[0].astype(F32) + below[1].astype(F32)).astype(BF)
+    down[...] = (stay[1].astype(F32) + above[1].astype(F32)).astype(BF)
+
+
+def sum_kernel(own, below, above, *refs):
+    total = own[...] + below[0].astype(F32) + above[0].astype(F32)
     for ref in refs[:-2]:
-        total = total + ref[...].astype(F32)
+        total = total + ref[...].reshape(total.shape).astype(F32)
     refs[-2][...] = total
     refs[-1][...] = total.astype(BF)
 
@@ -383,10 +395,10 @@
         (
             pltpu.HBM((PEERS, behind, TILE), BF),
             pltpu.HBM(triple, F32),
-            *[pltpu.HBM(triple, BF)] * (NZ - 1),
+            *[pltpu.HBM((size,) + triple, BF) for _, size in WAVES],
         ),
         [SMEM, SMEM, VMEM, VMEM],
-        [HBM] * (NZ + 1),
+        [HBM] * (len(WAVES) + 2),
         [
             pltpu.VMEM((per, TILE, 2 * TILE), BF),
             pltpu.VMEM((per, TILE, TILE), BF),
@@ -394,14 +406,16 @@
             pltpu.VMEM((per, TILE, TILE), F32),
             pltpu.VMEM((PEERS, behind, TILE), BF),
             pltpu.VMEM(triple, F32),
-            pltpu.VMEM((NZ,) + triple, BF),
+            pltpu.VMEM((NZ - 1,) + triple, BF),
             pltpu.SemaphoreType.DMA((PEERS // 8,)),
-            pltpu.SemaphoreType.DMA((NZ,)),
+            pltpu.SemaphoreType.DMA((len(WAVES) + 1,)),
         ],
     )(plan, place, got, weights)
     returned = exchange(back, ("expert", "x"))
     if lean(per):
-        ordered = jnp.roll(jnp.stack([term.astype(F32) for term in grads]), place[1], axis=0)
+        chunks = jnp.concatenate(grads[1:], axis=0)
+        chunks = [grads[0]] + [chunks[CHUNKS.index(shift)].astype(F32) for shift in range(1, NZ)]
+        ordered = jnp.roll(jnp.stack(chunks), place[1], axis=0)
         own = jnp.sum(exchange(ordered, "z"), axis=0)
         whole = exchange(jnp.broadcast_to(own[None], (NX,) + triple), "x")
         nearby = [
@@ -409,10 +423,15 @@
             for shift in range(1, NX)
         ]
     else:
-        terms = [moved(grads[shift], "z", shift) for shift in (1, 7, 2, 6, 3, 5, 4)]
+        kept, plus_one, minus_one, plus_two, stay = grads
+        below, above = moved(plus_one, "z", 1), moved(minus_one, "z", NZ - 1)
+        two = moved(plus_two, "z", 2)
+        up, down = call(relay_kernel, (shape(triple, BF),) * 2, [VMEM] * 3, (VMEM, VMEM))(
+            stay, below, above
+        )
         own, sent = call(
-            sum_kernel, (shape(triple, F32), shape(triple, BF)), [VMEM] * NZ, (VMEM, VMEM)
-        )(grads[0], *terms)
+            sum_kernel, (shape(triple, F32), shape(triple, BF)), [VMEM] * 6, (VMEM, VMEM)
+        )(kept, below, above, two, moved(up, "z", 3), moved(down, "z", NZ - 2))
         nearby = [moved(sent, "x", shift) for shift in range(1, NX)]
     token_grad, prob_grad = call(
         functools.partial(combine_kernel, per),

time: 109 us -> 111 us (1.018)
  starting transfers between devices: 41.7 us -> 38.5 us
  waiting for transfers between devices: 16.4 us -> 19.3 us
  Pallas kernels: 16.7 us -> 18.3 us
    all_to_all x3, waiting for transfers between devices: 5.38 us -> 10.4 us  [exchange(): return lax.all_to_all(values, axes, split_axis=0, concat_axis=0, tiled=True)]
    all_to_all x3, starting transfers between devices: 15.9 us -> 13.6 us  [exchange(): return lax.all_to_all(values, axes, split_axis=0, concat_axis=0, tiled=True)]
    ppermute x13 -> x11, waiting for transfers between devices: 11 us -> 8.99 us  [moved(): lax.ppermute(values, axis, [(i, (i + shift) % size) for i in range(size)])]
    pallas_call x1, Pallas kernels: 6.18 us -> 7.36 us  [rest(): call(functools.partial(expert_kernel, per), (pltpu.HBM((PEERS, behind, TI...]
    ppermute x13 -> x11, starting transfers between devices: 25.8 us -> 24.9 us  [moved(): lax.ppermute(values, axis, [(i, (i + shift) % size) for i in range(size)])]
  transfers between devices with their start and end apart: 16 -> 14, of which waited for: 3 -> 5; matrix products, arithmetic and copies ran while one was open for 1% -> 1% of each run, Pallas kernels for 4% -> 4%
where the time goes in v1:
time: 111 us; the launch traced here: 110 us
  starting transfers between devices  38.5 us (35%)
  blocking collectives  28.8 us (26%)
  waiting for transfers between devices  19.3 us (17%)
  Pallas kernels  18.3 us (16%)
  other arithmetic  2.23 us (2%)
  local copies, waits for them, and re-layouts  1.46 us (1%)
  between operations  1.32 us (1%)
    all_gather x1, blocking collectives, rest(): weights = lax.all_gather(weights, 'z', axis=0, tiled=True)  28.8 us
    ppermute x11, starting transfers between devices, moved(): lax.ppermute(values, axis, [(i, (i + shift) % size) for i in range(size)])  24.9 us
    all_to_all x3, starting transfers between devices, exchange(): return lax.all_to_all(values, axes, split_axis=0, concat_axis=0, tiled=True)  13.6 us
    all_to_all x3, waiting for transfers between devices, exchange(): return lax.all_to_all(values, axes, split_axis=0, concat_axis=0, tiled=True)  10.4 us
    ppermute x11, waiting for transfers between devices, moved(): lax.ppermute(values, axis, [(i, (i + shift) % size) for i in range(size)])  8.99 us
    pallas_call x1, Pallas kernels, rest(): call(functools.partial(expert_kernel, per), (pltpu.HBM((PEERS, behind, TI...  7.36 us
    pallas_call x1, Pallas kernels, rest(): call(functools.partial(dispatch_kernel, per), pltpu.HBM((PEERS, ahead, TI...  4.39 us
    pallas_call x1, Pallas kernels, rest(): call(functools.partial(combine_kernel, per), (shape((ROWS, WIDTH), BF), s...  3.73 us
  transfers between devices with their start and end apart: 14, of which 5 were waited for; matrix products, arithmetic and copies ran while one was open for 1% of the time, Pallas kernels for 4%

profile of v1, /device:TPU:32, one launch (start us, length us, event | category | flops | bytes accessed | tf_op | source)
XLA Modules:
  0.0 110.3 jit_solution(9257653029729141724)
XLA Ops:
  2.9 1.6 %collective-permute-start.16 = (bf16[3,128,128]{2,1,0:T(8,128)(2,1)S(1)}, bf16[3,128,128]{2,1,0:T(8,128)(2,1)S(1)}, u32[]{:S(2)}, u32[]{:S(2)}) collective-permute-start(bf16[3,128,128]{2,1,0:T(8,128)(2,1)S(1)} %pad_maximum_fusion), channel_id=1, source_target_pairs={{0,8},{8,16},{16,24},{24,0},{1,9},{9,17},{17,25},{25,1},{2,10},{10... | collective-permute-start | bytes 294920 | tf_op jit(solution)/shard_map/ppermute | solution.py:363
  4.5 2.7 %collective-permute-start.17 = (bf16[3,128,128]{2,1,0:T(8,128)(2,1)S(1)}, bf16[3,128,128]{2,1,0:T(8,128)(2,1)S(1)}, u32[]{:S(2)}, u32[]{:S(2)}) collective-permute-start(bf16[3,128,128]{2,1,0:T(8,128)(2,1)S(1)} %pad_maximum_fusion), channel_id=1, source_target_pairs={{0,16},{8,24},{16,0},{24,8},{1,17},{9,25},{17,1},{25,9},{2,18},{10... | collective-permute-start | bytes 294920 | tf_op jit(solution)/shard_map/ppermute | solution.py:363
  7.2 1.4 %collective-permute-start.18 = (bf16[3,128,128]{2,1,0:T(8,128)(2,1)S(1)}, bf16[3,128,128]{2,1,0:T(8,128)(2,1)S(1)}, u32[]{:S(2)}, u32[]{:S(2)}) collective-permute-start(bf16[3,128,128]{2,1,0:T(8,128)(2,1)S(1)} %pad_maximum_fusion), channel_id=1, source_target_pairs={{0,24},{8,0},{16,8},{24,16},{1,25},{9,1},{17,9},{25,17},{2,26},{10... | collective-permute-start | bytes 294920 | tf_op jit(solution)/shard_map/ppermute | solution.py:363
  8.6 4.5 %all-to-all-start.8 = ((s32[8,8,128]{2,1,0:T(8,128)}), s32[8,8,128]{2,1,0:T(8,128)S(1)}, u32[]{:S(2)}, u32[]{:S(2)}) async-start(s32[8,8,128]{2,1,0:T(8,128)} %get-tuple-element.174), calls=%async_computation.8 | async-start | bytes 65536 | tf_op jit(solution)/shard_map/all_to_all | solution.py:358
  13.2 5.4 %all-to-all-done.8 = s32[8,8,128]{2,1,0:T(8,128)S(1)} async-done(((s32[8,8,128]{2,1,0:T(8,128)}), s32[8,8,128]{2,1,0:T(8,128)S(1)}, u32[]{:S(2)}, u32[]{:S(2)}) %all-to-all-start.8) | async-done | bytes 32800 | tf_op jit(solution)/shard_map/all_to_all | solution.py:358
  19.9 89.9 %conditional.1 = (bf16[128,3072]{1,0:T(8,128)(2,1)}, bf16[2,128]{1,0:T(2,128)(2,1)S(1)}, f32[1,1,128,128]{3,2,1,0:T(8,128)}, f32[1,1,128,128]{3,2,1,0:T(8,128)}, f32[1,1,128,128]{3,2,1,0:T(8,128)}) conditional(s32[]{:T(128)} %clamp.3, (s32[8,8,128]{2,1,0:T(8,128)S(1)}, s32[2,128]{1,0:T(2,128)}, bf16[2,128]{1,0:T(2,128)(2,1)}, ...), branch_computations={%region_1.0_spmd, %region_2.0_spmd, %region_3.5_spmd} | conditional | flops 252690432 | bytes 60330928 | solution.py:488
  20.1 4.4 %branch_1_fun.7 = bf16[32,336,128]{2,1,0:T(8,128)(2,1)} custom-call(s32[8,8,128]{2,1,0:T(8,128)S(1)} %get-tuple-element.100.plans, s32[2,128]{1,0:T(2,128)} %get-tuple-element.101.ids, bf16[2,128]{1,0:T(2,128)(2,1)} %get-tuple-element.104.probs, bf16[128,3072]{1,0:T(8,128)(2,1)} %get-tuple-element.105.tokens, bf16[128,3072]{1,0:T(8,128)(2,1)} %get-tuple-element.106.cot), custom_call_target="tpu_custom_call" | custom-call | tf_op jit(solution)/shard_map/cond/branch_1_fun/pallas_call | solution.py:371
  24.5 4.1 %all-to-all-start.2 = ((bf16[32,336,128]{2,1,0:T(8,128)(2,1)}), bf16[32,336,128]{2,1,0:T(8,128)(2,1)S(1)}, u32[]{:S(2)}, u32[]{:S(2)}) async-start(bf16[32,336,128]{2,1,0:T(8,128)(2,1)} %branch_1_fun.7), calls=%async_computation.2 | async-start | bytes 5505024 | tf_op jit(solution)/shard_map/cond/branch_1_fun/all_to_all | solution.py:358
  29.3 28.8 %all_gather.7.weights = bf16[24,128,128]{2,1,0:T(8,128)(2,1)S(1)} all-gather(bf16[3,128,128]{2,1,0:T(8,128)(2,1)S(1)} %branch_1_fun.8), channel_id=1, replica_groups=mesh['expert'=8,'x'=4,'z'=8] {'z'}, dimensions={0}, use_global_device_ids=true | all-gather | bytes 884736 | tf_op jit(solution)/shard_map/cond/branch_1_fun/all_gather | solution.py:392
  58.0 5.0 %all-to-all-done.2.got = bf16[32,336,128]{2,1,0:T(8,128)(2,1)S(1)} async-done(((bf16[32,336,128]{2,1,0:T(8,128)(2,1)}), bf16[32,336,128]{2,1,0:T(8,128)(2,1)S(1)}, u32[]{:S(2)}, u32[]{:S(2)}) %all-to-all-start.2) | async-done | bytes 2752544 | tf_op jit(solution)/shard_map/cond/branch_1_fun/all_to_all | solution.py:358
  63.0 7.4 %branch_1_fun.9 = (bf16[32,176,128]{2,1,0:T(8,128)(2,1)}, f32[3,128,128]{2,1,0:T(8,128)}, bf16[2,3,128,128]{3,2,1,0:T(8,128)(2,1)}, bf16[2,3,128,128]{3,2,1,0:T(...) custom-call(s32[8,128]{1,0:T(8,128)S(1)} %get-tuple-element.102.plan, ...), custom_call_target="tpu_custom_call" | custom-call | tf_op jit(solution)/shard_map/cond/branch_1_fun/pallas_call | solution.py:393
  70.4 5.1 %all-to-all-start.3 = ((bf16[32,176,128]{2,1,0:T(8,128)(2,1)}), bf16[32,176,128]{2,1,0:T(8,128)(2,1)S(1)}, u32[]{:S(2)}, u32[]{:S(2)}) async-start(bf16[32,176,128]{2,1,0:T(8,128)(2,1)} %get-tuple-element.111), calls=%async_computation.3 | async-start | bytes 2883584 | tf_op jit(solution)/shard_map/cond/branch_1_fun/all_to_all | solution.py:358
  75.5 2.0 %collective-permute-start.8 = (bf16[2,3,128,128]{3,2,1,0:T(8,128)(2,1)}, bf16[2,3,128,128]{3,2,1,0:T(8,128)(2,1)S(1)}, u32[]{:S(2)}, u32[]{:S(2)}) collective-permute-start(bf16[2,3,128,128]{3,2,1,0:T(8,128)(2,1)} %get-tuple-element.114), channel_id=1, source_target_pairs={{0,1},{1,2},{2,3},{3,4},{4,5},{5,6},{6,7},{7,0},{8,9},{9,10},{10,1... | collective-permute-start | bytes 589832 | tf_op jit(solution)/shard_map/cond/branch_1_fun/ppermute | solution.py:363
  77.6 4.4 %collective-permute-start.10 = (bf16[1,3,128,128]{3,2,1,0:T(8,128)(2,1)}, bf16[1,3,128,128]{3,2,1,0:T(8,128)(2,1)S(1)}, u32[]{:S(2)}, u32[]{:S(2)}) collective-permute-start(bf16[1,3,128,128]{3,2,1,0:T(8,128)(2,1)} %get-tuple-element.116), channel_id=1, source_target_pairs={{0,2},{1,3},{2,4},{3,5},{4,6},{5,7},{6,0},{7,1},{8,10},{9,11},{10,... | collective-permute-start | bytes 294920 | tf_op jit(solution)/shard_map/cond/branch_1_fun/ppermute | solution.py:363
  82.0 2.7 %collective-permute-done.8.below = bf16[2,3,128,128]{3,2,1,0:T(8,128)(2,1)S(1)} collective-permute-done((bf16[2,3,128,128]{3,2,1,0:T(8,128)(2,1)}, bf16[2,3,128,128]{3,2,1,0:T(8,128)(2,1)S(1)}, u32[]{:S(2)}, u32[]{:S(2)}) %collective-permute-start.8) | collective-permute-done | bytes 196640 | tf_op jit(solution)/shard_map/cond/branch_1_fun/ppermute | solution.py:363
  84.6 0.9 copy-done.3
  85.6 6.7 %collective-permute-start.11 = (bf16[3,128,128]{2,1,0:T(8,128)(2,1)S(1)}, bf16[3,128,128]{2,1,0:T(8,128)(2,1)S(1)}, u32[]{:S(2)}, u32[]{:S(2)}) collective-permute-start(bf16[3,128,128]{2,1,0:T(8,128)(2,1)S(1)} %get-tuple-element.118), channel_id=1, source_target_pairs={{0,3},{1,4},{2,5},{3,6},{4,7},{5,0},{6,1},{7,2},{8,11},{9,12},{10,... | collective-permute-start | bytes 294920 | tf_op jit(solution)/shard_map/cond/branch_1_fun/ppermute | solution.py:363
  92.4 5.2 %collective-permute-done.11.refs_1_ = bf16[3,128,128]{2,1,0:T(8,128)(2,1)S(1)} collective-permute-done((bf16[3,128,128]{2,1,0:T(8,128)(2,1)S(1)}, bf16[3,128,128]{2,1,0:T(8,128)(2,1)S(1)}, u32[]{:S(2)}, u32[]{:S(2)}) %collective-permute-start.11) | collective-permute-done | bytes 98336 | tf_op jit(solution)/shard_map/cond/branch_1_fun/ppermute | solution.py:363
  97.6 1.1 collective-permute-done.12.refs_2_
  98.8 1.8 %collective-permute-start.13 = (bf16[3,128,128]{2,1,0:T(8,128)(2,1)S(1)}, bf16[3,128,128]{2,1,0:T(8,128)(2,1)S(1)}, u32[]{:S(2)}, u32[]{:S(2)}) collective-permute-start(bf16[3,128,128]{2,1,0:T(8,128)(2,1)S(1)} %get-tuple-element.120), channel_id=1, source_target_pairs={{0,8},{8,16},{16,24},{24,0},{1,9},{9,17},{17,25},{25,1},{2,10},{10... | collective-permute-start | bytes 294920 | tf_op jit(solution)/shard_map/cond/branch_1_fun/ppermute | solution.py:363
  100.6 2.7 %collective-permute-start.14 = (bf16[3,128,128]{2,1,0:T(8,128)(2,1)S(1)}, bf16[3,128,128]{2,1,0:T(8,128)(2,1)S(1)}, u32[]{:S(2)}, u32[]{:S(2)}) collective-permute-start(bf16[3,128,128]{2,1,0:T(8,128)(2,1)S(1)} %get-tuple-element.120), channel_id=1, source_target_pairs={{0,16},{8,24},{16,0},{24,8},{1,17},{9,25},{17,1},{25,9},{2,18},{10... | collective-permute-start | bytes 294920 | tf_op jit(solution)/shard_map/cond/branch_1_fun/ppermute | solution.py:363
  103.2 1.5 %collective-permute-start.15 = (bf16[3,128,128]{2,1,0:T(8,128)(2,1)S(1)}, bf16[3,128,128]{2,1,0:T(8,128)(2,1)S(1)}, u32[]{:S(2)}, u32[]{:S(2)}) collective-permute-start(bf16[3,128,128]{2,1,0:T(8,128)(2,1)S(1)} %get-tuple-element.120), channel_id=1, source_target_pairs={{0,24},{8,0},{16,8},{24,16},{1,25},{9,1},{17,9},{25,17},{2,26},{10... | collective-permute-start | bytes 294920 | tf_op jit(solution)/shard_map/cond/branch_1_fun/ppermute | solution.py:363
  104.7 3.7 %branch_1_fun.10 = (bf16[128,3072]{1,0:T(8,128)(2,1)}, bf16[2,128]{1,0:T(2,128)(2,1)S(1)}) custom-call(s32[8,8,128]{2,1,0:T(8,128)S(1)} %copy-done.5, s32[2,128]{1,0:T(2,128)S(1)} %copy-done.13, bf16[32,176,128]{2,1,0:T(8,128)(2,1)S(1)} %all-to-all-done.3.back), custom_call_target="tpu_custom_call" | custom-call | flops 251658240 | bytes 13238272 | tf_op jit(solution)/shard_map/cond/branch_1_fun/pallas_call | solution.py:436
  108.5 1.3 %branch_1_fun.13 = (f32[1,1,128,128]{3,2,1,0:T(8,128)}, f32[1,1,128,128]{3,2,1,0:T(8,128)}, f32[1,1,128,128]{3,2,1,0:T(8,128)}) custom-call(s32[8,128]{1,0:T(8,128)S(1)} %get-tuple-element.102.plan, s32[2]{0:T(128)S(1)} %get-tuple-element.103.place, f32[3,128,128]{2,1,0:T(8,128)S(1)} %get-tuple-element.123.own, ...), custom_call_target="tpu_custom_call" | custom-call | tf_op jit(solution)/shard_map/cond/branch_1_fun/pallas_call | solution.py:450
  (30 shorter events, 4.5 us)
Async XLA Ops:
  2.9 16.9 %collective-permute-start.16 = (bf16[3,128,128]{2,1,0:T(8,128)(2,1)S(1)}, bf16[3,128,128]{2,1,0:T(8,128)(2,1)S(1)}, u32[]{:S(2)}, u32[]{:S(2)}) collective-permute-start(bf16[3,128,128]{2,1,0:T(8,128)(2,1)S(1)} %pad_maximum_fusion), channel_id=1, source_target_pairs={{0,8},{8,16},{16,24},{24,0},{1,9},{9,17},{17,25},{25,1},{2,10},{10... | collective-permute-start | bytes 294920 | tf_op jit(solution)/shard_map/ppermute | solution.py:363
  4.5 15.4 %collective-permute-start.17 = (bf16[3,128,128]{2,1,0:T(8,128)(2,1)S(1)}, bf16[3,128,128]{2,1,0:T(8,128)(2,1)S(1)}, u32[]{:S(2)}, u32[]{:S(2)}) collective-permute-start(bf16[3,128,128]{2,1,0:T(8,128)(2,1)S(1)} %pad_maximum_fusion), channel_id=1, source_target_pairs={{0,16},{8,24},{16,0},{24,8},{1,17},{9,25},{17,1},{25,9},{2,18},{10... | collective-permute-start | bytes 294920 | tf_op jit(solution)/shard_map/ppermute | solution.py:363
  7.2 12.7 %collective-permute-start.18 = (bf16[3,128,128]{2,1,0:T(8,128)(2,1)S(1)}, bf16[3,128,128]{2,1,0:T(8,128)(2,1)S(1)}, u32[]{:S(2)}, u32[]{:S(2)}) collective-permute-start(bf16[3,128,128]{2,1,0:T(8,128)(2,1)S(1)} %pad_maximum_fusion), channel_id=1, source_target_pairs={{0,24},{8,0},{16,8},{24,16},{1,25},{9,1},{17,9},{25,17},{2,26},{10... | collective-permute-start | bytes 294920 | tf_op jit(solution)/shard_map/ppermute | solution.py:363
  8.6 9.9 %all-to-all-start.8 = ((s32[8,8,128]{2,1,0:T(8,128)}), s32[8,8,128]{2,1,0:T(8,128)S(1)}, u32[]{:S(2)}, u32[]{:S(2)}) async-start(s32[8,8,128]{2,1,0:T(8,128)} %get-tuple-element.174), calls=%async_computation.8 | async-start | bytes 65536 | tf_op jit(solution)/shard_map/all_to_all | solution.py:358
  20.1 4.4 %copy-start.4 = (s32[8,8,128]{2,1,0:T(8,128)}, s32[8,8,128]{2,1,0:T(8,128)S(1)}, u32[]{:S(2)}) copy-start(s32[8,8,128]{2,1,0:T(8,128)S(1)} %get-tuple-element.100.plans) | copy-start | bytes 98308 | tf_op jit(solution)/shard_map/cond
  24.5 38.5 %all-to-all-start.2 = ((bf16[32,336,128]{2,1,0:T(8,128)(2,1)}), bf16[32,336,128]{2,1,0:T(8,128)(2,1)S(1)}, u32[]{:S(2)}, u32[]{:S(2)}) async-start(bf16[32,336,128]{2,1,0:T(8,128)(2,1)} %branch_1_fun.7), calls=%async_computation.2 | async-start | bytes 5505024 | tf_op jit(solution)/shard_map/cond/branch_1_fun/all_to_all | solution.py:358
  58.0 46.7 %copy-start.13 = (s32[2,128]{1,0:T(2,128)S(1)}, s32[2,128]{1,0:T(2,128)}, u32[]{:S(2)}) copy-start(s32[2,128]{1,0:T(2,128)} %get-tuple-element.101.ids) | copy-start | bytes 3076 | tf_op jit(solution)/shard_map/cond
  70.4 28.3 %copy-start.1 = (f32[3,128,128]{2,1,0:T(8,128)S(1)}, f32[3,128,128]{2,1,0:T(8,128)}, u32[]{:S(2)}) copy-start(f32[3,128,128]{2,1,0:T(8,128)} %get-tuple-element.113.own) | copy-start | bytes 589828 | tf_op jit(solution)/shard_map/cond
  70.4 34.3 %copy-start.5 = (s32[8,8,128]{2,1,0:T(8,128)S(1)}, s32[8,8,128]{2,1,0:T(8,128)}, u32[]{:S(2)}) copy-start(s32[8,8,128]{2,1,0:T(8,128)} %copy-done.4) | copy-start | bytes 98308 | tf_op jit(solution)/shard_map/cond
  70.4 34.3 %all-to-all-start.3 = ((bf16[32,176,128]{2,1,0:T(8,128)(2,1)}), bf16[32,176,128]{2,1,0:T(8,128)(2,1)S(1)}, u32[]{:S(2)}, u32[]{:S(2)}) async-start(bf16[32,176,128]{2,1,0:T(8,128)(2,1)} %get-tuple-element.111), calls=%async_computation.3 | async-start | bytes 2883584 | tf_op jit(solution)/shard_map/cond/branch_1_fun/all_to_all | solution.py:358
  75.5 9.2 %collective-permute-start.8 = (bf16[2,3,128,128]{3,2,1,0:T(8,128)(2,1)}, bf16[2,3,128,128]{3,2,1,0:T(8,128)(2,1)S(1)}, u32[]{:S(2)}, u32[]{:S(2)}) collective-permute-start(bf16[2,3,128,128]{3,2,1,0:T(8,128)(2,1)} %get-tuple-element.114), channel_id=1, source_target_pairs={{0,1},{1,2},{2,3},{3,4},{4,5},{5,6},{6,7},{7,0},{8,9},{9,10},{10,1... | collective-permute-start | bytes 589832 | tf_op jit(solution)/shard_map/cond/branch_1_fun/ppermute | solution.py:363
  77.5 7.2 %collective-permute-start.9 = (bf16[2,3,128,128]{3,2,1,0:T(8,128)(2,1)}, bf16[2,3,128,128]{3,2,1,0:T(8,128)(2,1)S(1)}, u32[]{:S(2)}, u32[]{:S(2)}) collective-permute-start(bf16[2,3,128,128]{3,2,1,0:T(8,128)(2,1)} %get-tuple-element.115), channel_id=1, source_target_pairs={{0,7},{1,0},{2,1},{3,2},{4,3},{5,4},{6,5},{7,6},{8,15},{9,8},{10,9... | collective-permute-start | bytes 589832 | tf_op jit(solution)/shard_map/cond/branch_1_fun/ppermute | solution.py:363
  77.6 14.8 %collective-permute-start.10 = (bf16[1,3,128,128]{3,2,1,0:T(8,128)(2,1)}, bf16[1,3,128,128]{3,2,1,0:T(8,128)(2,1)S(1)}, u32[]{:S(2)}, u32[]{:S(2)}) collective-permute-start(bf16[1,3,128,128]{3,2,1,0:T(8,128)(2,1)} %get-tuple-element.116), channel_id=1, source_target_pairs={{0,2},{1,3},{2,4},{3,5},{4,6},{5,7},{6,0},{7,1},{8,10},{9,11},{10,... | collective-permute-start | bytes 294920 | tf_op jit(solution)/shard_map/cond/branch_1_fun/ppermute | solution.py:363
  84.6 0.9 copy-start.3
  85.6 12.0 %collective-permute-start.11 = (bf16[3,128,128]{2,1,0:T(8,128)(2,1)S(1)}, bf16[3,128,128]{2,1,0:T(8,128)(2,1)S(1)}, u32[]{:S(2)}, u32[]{:S(2)}) collective-permute-start(bf16[3,128,128]{2,1,0:T(8,128)(2,1)S(1)} %get-tuple-element.118), channel_id=1, source_target_pairs={{0,3},{1,4},{2,5},{3,6},{4,7},{5,0},{6,1},{7,2},{8,11},{9,12},{10,... | collective-permute-start | bytes 294920 | tf_op jit(solution)/shard_map/cond/branch_1_fun/ppermute | solution.py:363
  92.3 6.4 %collective-permute-start.12 = (bf16[3,128,128]{2,1,0:T(8,128)(2,1)S(1)}, bf16[3,128,128]{2,1,0:T(8,128)(2,1)S(1)}, u32[]{:S(2)}, u32[]{:S(2)}) collective-permute-start(bf16[3,128,128]{2,1,0:T(8,128)(2,1)S(1)} %get-tuple-element.119), channel_id=1, source_target_pairs={{0,6},{1,7},{2,0},{3,1},{4,2},{5,3},{6,4},{7,5},{8,14},{9,15},{10,... | collective-permute-start | bytes 294920 | tf_op jit(solution)/shard_map/cond/branch_1_fun/ppermute | solution.py:363
  98.8 9.7 %collective-permute-start.13 = (bf16[3,128,128]{2,1,0:T(8,128)(2,1)S(1)}, bf16[3,128,128]{2,1,0:T(8,128)(2,1)S(1)}, u32[]{:S(2)}, u32[]{:S(2)}) collective-permute-start(bf16[3,128,128]{2,1,0:T(8,128)(2,1)S(1)} %get-tuple-element.120), channel_id=1, source_target_pairs={{0,8},{8,16},{16,24},{24,0},{1,9},{9,17},{17,25},{25,1},{2,10},{10... | collective-permute-start | bytes 294920 | tf_op jit(solution)/shard_map/cond/branch_1_fun/ppermute | solution.py:363
  100.6 7.9 %collective-permute-start.14 = (bf16[3,128,128]{2,1,0:T(8,128)(2,1)S(1)}, bf16[3,128,128]{2,1,0:T(8,128)(2,1)S(1)}, u32[]{:S(2)}, u32[]{:S(2)}) collective-permute-start(bf16[3,128,128]{2,1,0:T(8,128)(2,1)S(1)} %get-tuple-element.120), channel_id=1, source_target_pairs={{0,16},{8,24},{16,0},{24,8},{1,17},{9,25},{17,1},{25,9},{2,18},{10... | collective-permute-start | bytes 294920 | tf_op jit(solution)/shard_map/cond/branch_1_fun/ppermute | solution.py:363
  103.2 5.2 %collective-permute-start.15 = (bf16[3,128,128]{2,1,0:T(8,128)(2,1)S(1)}, bf16[3,128,128]{2,1,0:T(8,128)(2,1)S(1)}, u32[]{:S(2)}, u32[]{:S(2)}) collective-permute-start(bf16[3,128,128]{2,1,0:T(8,128)(2,1)S(1)} %get-tuple-element.120), channel_id=1, source_target_pairs={{0,24},{8,0},{16,8},{24,16},{1,25},{9,1},{17,9},{25,17},{2,26},{10... | collective-permute-start | bytes 294920 | tf_op jit(solution)/shard_map/cond/branch_1_fun/ppermute | solution.py:363
  109.8 0.5 copy-start.15
